TPU v7x, 32 devices: a whole 2x2x4 slice. The times are simulated.
32 devices in a mesh: dp: 16 (over z, x, core), tensor: 2 (over y).
Axes of the slice: x: 2, y: 2, z: 4, core: 2. Of those that a mesh axis runs over, the one named last changes fastest.
Arguments:
- tokens: bfloat16 [8192, 1280], P(('dp', 'tensor')), may hold values from -6 to 6
- w_query: bfloat16 [1280, 1280], P('dp', 'tensor'), may hold values from -0.15625 to 0.15625
- w_key: bfloat16 [1280, 1280], P('dp', 'tensor'), may hold values from -0.15625 to 0.15625
- w_value: bfloat16 [1280, 1280], P('dp', 'tensor'), may hold values from -0.15625 to 0.15625
- w_output: bfloat16 [1280, 1280], P('tensor', 'dp'), may hold values from -0.625 to 0.625
- w_in: bfloat16 [1280, 1280], P('dp', 'tensor'), may hold values from -0.15625 to 0.15625
- w_out: bfloat16 [1280, 1280], P('tensor', 'dp'), may hold values from -0.15625 to 0.15625
- gain_attn: bfloat16 [1280], P('dp'), may hold values from 0.5 to 1.5
- gain_mlp: bfloat16 [1280], P('dp'), may hold values from 0.5 to 1.5
- seq_lengths: int32 [16, 5], P('dp'), may hold values from 1 to 384, as said below
- seq_offsets: int32 [16, 5], P('dp'), may hold values from 0 to 511, as said below
- cotangent: bfloat16 [8192, 1280], P(('dp', 'tensor')), may hold values from -6 to 6
Outputs:
- mixed: bfloat16 [8192, 1280], P(('dp', 'tensor'))
- grad_tokens: float32 [8192, 1280], P(('dp', 'tensor'))
- grad_w_query: float32 [1280, 1280], P('dp', 'tensor')
- grad_w_key: float32 [1280, 1280], P('dp', 'tensor')
- grad_w_value: float32 [1280, 1280], P('dp', 'tensor')
- grad_w_output: float32 [1280, 1280], P('tensor', 'dp')
- grad_w_in: float32 [1280, 1280], P('dp', 'tensor')
- grad_w_out: float32 [1280, 1280], P('tensor', 'dp')
- grad_gain_attn: float32 [1280], P('dp')
- grad_gain_mlp: float32 [1280], P('dp')
Inputs may be any that keep to these rules, and one draw needn't show every extreme that they name: `seq_lengths`: every slot holds a series of at least one row; the series of a group lie in disjoint row ranges, in slot order; the longest is reached in some group. `seq_offsets`: the first row of each slot's series within its group; rows in no series are padding.
All inputs are finite; a program needn't handle non-finite values.
Results may differ from a plain program's by a relative error of at most 0.012.
Values may be sent and summed in bfloat16 or wider, within the bound.
No kernel may reach another device: no remote copies, remote signals or barrier semaphores. Data moves between devices by JAX's collectives and lax.ppermute only.
A program may use at most 192 MiB of HBM per device.

v0:
```python
import jax
import jax.numpy as jnp
from jax import lax
from jax.sharding import PartitionSpec as P

HEAD_DIM = 80


highest = lax.Precision.HIGHEST
epsilon = 1e-06
stat_eps = 1e-05
masked_score = -1e30
contract_last = (((1,), (1,)), ((), ()))
contract_first = (((0,), (0,)), ((), ()))


def against(left, right):
    return lax.dot_general(left, right, contract_last, preferred_element_type=jnp.float32)


def across(left, right):
    return lax.dot_general(left, right, contract_first, preferred_element_type=jnp.float32)


def row_layout(lengths, offsets, group_rows):
    row_ids = jnp.arange(group_rows, dtype=jnp.int32)
    inside = (row_ids[:, None] >= offsets[None, :]) & (
        row_ids[:, None] < offsets[None, :] + lengths[None, :]
    )
    member = inside.astype(jnp.float32)
    slot_ids = jnp.arange(offsets.shape[0], dtype=jnp.int32)
    segment = jnp.sum(jnp.where(inside, slot_ids[None, :] + 1, 0), axis=1) - 1
    seq_start = jnp.sum(jnp.where(inside, offsets[None, :], 0), axis=1)
    position = jnp.where(segment >= 0, row_ids - seq_start, 0).astype(jnp.float32)
    first_rows = (row_ids[:, None] == offsets[None, :]).astype(jnp.float32)
    return (member, segment, position, first_rows)


def rotary_tables(position):
    half_dim = HEAD_DIM // 2
    freqs = 10000.0 ** (-2.0 * jnp.arange(half_dim, dtype=jnp.float32) / HEAD_DIM)
    angles = position[:, None] * freqs[None, :]
    return (jnp.cos(angles), jnp.sin(angles))


def rotate(values, cosine, sine, direction):
    row_count = values.shape[0]
    shaped = values.reshape(row_count, -1, HEAD_DIM)
    half_dim = HEAD_DIM // 2
    first_half = shaped[..., :half_dim]
    second_half = shaped[..., half_dim:]
    cos_b = cosine[:, None, :]
    sin_b = sine[:, None, :] * direction
    turned = jnp.concatenate(
        [first_half * cos_b - second_half * sin_b, first_half * sin_b + second_half * cos_b],
        axis=-1,
    )
    return turned.reshape(row_count, -1)


def rms_norm(values):
    factor = lax.rsqrt(jnp.mean(values * values, axis=-1, keepdims=True) + epsilon)
    return (values * factor, factor)


def norm_back(grad_normed, normed, factor):
    return factor * (grad_normed - normed * jnp.mean(grad_normed * normed, axis=-1, keepdims=True))


def allowed_mask(seg_query, query_ids, segment, key_ids):
    same = (
        (seg_query[:, None] == segment[None, :])
        & (key_ids[None, :] <= query_ids[:, None])
        & (seg_query[:, None] >= 0)
    )
    return same | (query_ids[:, None] == key_ids[None, :])


def block_scores(query_all, key_all, segment, row_begin, block_rows):
    group_rows = key_all.shape[0]
    key_ids = jnp.arange(group_rows, dtype=jnp.int32)
    query_ids = row_begin + jnp.arange(block_rows, dtype=jnp.int32)
    queries = lax.dynamic_slice_in_dim(query_all, row_begin, block_rows, 0)
    scores = jnp.einsum(
        "qhd,khd->hqk", queries, key_all, preferred_element_type=jnp.float32
    ) * HEAD_DIM ** (-0.5)
    seg_query = lax.dynamic_slice_in_dim(segment, row_begin, block_rows, 0)
    mask = allowed_mask(seg_query, query_ids, segment, key_ids)
    return (jnp.where(mask[None], scores, masked_score), queries)


def attention_forward(q_rot, k_rot, values, segment):
    group_rows, head_width = q_rot.shape
    block_rows = min(512, group_rows)
    query_all = q_rot.reshape(group_rows, -1, HEAD_DIM)
    key_all = k_rot.reshape(group_rows, -1, HEAD_DIM)
    value_all = values.reshape(group_rows, -1, HEAD_DIM)

    def one_block(block_index):
        scores, queries = block_scores(
            query_all, key_all, segment, block_index * block_rows, block_rows
        )
        top = jnp.max(scores, axis=-1, keepdims=True)
        expo = jnp.exp(scores - top)
        total_exp = jnp.sum(expo, axis=-1, keepdims=True)
        probs = (expo / total_exp).astype(jnp.bfloat16)
        heads = jnp.einsum("hqk,khd->qhd", probs, value_all, preferred_element_type=jnp.float32)
        return (heads.reshape(block_rows, head_width), (top + jnp.log(total_exp))[..., 0])

    outs, log_sums = lax.map(one_block, jnp.arange(group_rows // block_rows, dtype=jnp.int32))
    return (outs.reshape(group_rows, head_width), log_sums)


def attention_backward(q_rot, k_rot, values, segment, log_sums, heads_grad):
    group_rows, head_width = q_rot.shape
    block_rows = min(512, group_rows)
    query_all = q_rot.reshape(group_rows, -1, HEAD_DIM)
    key_all = k_rot.reshape(group_rows, -1, HEAD_DIM)
    value_all = values.reshape(group_rows, -1, HEAD_DIM)
    grad_all = heads_grad.reshape(group_rows, -1, HEAD_DIM)
    scale_factor = HEAD_DIM ** (-0.5)

    def one_block(carry, block_index):
        key_grad, value_grad = carry
        row_begin = block_index * block_rows
        scores, queries = block_scores(query_all, key_all, segment, row_begin, block_rows)
        probs = jnp.exp(scores - log_sums[block_index][..., None])
        grads_block = lax.dynamic_slice_in_dim(grad_all, row_begin, block_rows, 0)
        prob_grad = jnp.einsum(
            "qhd,khd->hqk", grads_block, value_all, preferred_element_type=jnp.float32
        )
        inner = jnp.sum(probs * prob_grad, axis=-1, keepdims=True)
        score_grad = (probs * (prob_grad - inner)).astype(jnp.bfloat16)
        query_grad = (
            jnp.einsum("hqk,khd->qhd", score_grad, key_all, preferred_element_type=jnp.float32)
            * scale_factor
        )
        key_grad = (
            key_grad
            + jnp.einsum("hqk,qhd->khd", score_grad, queries, preferred_element_type=jnp.float32)
            * scale_factor
        )
        value_grad = value_grad + jnp.einsum(
            "hqk,qhd->khd",
            probs.astype(jnp.bfloat16),
            grads_block,
            preferred_element_type=jnp.float32,
        )
        return ((key_grad, value_grad), query_grad.reshape(block_rows, head_width))

    zeros = jnp.zeros(query_all.shape, jnp.float32)
    (key_grad, value_grad), query_grads = lax.scan(
        one_block, (zeros, zeros), jnp.arange(group_rows // block_rows, dtype=jnp.int32)
    )
    return (
        query_grads.reshape(group_rows, head_width),
        key_grad.reshape(group_rows, head_width),
        value_grad.reshape(group_rows, head_width),
    )


def split_weights(rows_full, columns_full, gains_full, head_width):
    qkv_width = 3 * head_width
    return (
        rows_full[:, :qkv_width],
        rows_full[:, qkv_width:],
        columns_full[:head_width],
        columns_full[head_width:],
        gains_full[0].astype(jnp.float32),
        gains_full[1].astype(jnp.float32),
    )


def local(
    tokens,
    w_query,
    w_key,
    w_value,
    w_output,
    w_in,
    w_out,
    gain_attn,
    gain_mlp,
    seq_lengths,
    seq_offsets,
    cotangent,
):
    own_rows = tokens.shape[0]
    feature_count = tokens.shape[1]
    head_width = w_query.shape[1]
    qkv_width = 3 * head_width
    row_blocks = jnp.concatenate([w_query, w_key, w_value, w_in], axis=1)
    column_blocks = jnp.concatenate([w_output, w_out], axis=0)
    gain_pair = jnp.stack([gain_attn, gain_mlp])
    rows_full, columns_full, gains_full = (
        lax.all_gather(row_blocks, "dp", axis=0, tiled=True),
        lax.all_gather(column_blocks, "dp", axis=1, tiled=True),
        lax.all_gather(gain_pair, "dp", axis=1, tiled=True),
    )
    w_qkv_full, w_in_full, w_output_full, w_out_full, gain_in, gain_mid = split_weights(
        rows_full, columns_full, gains_full, head_width
    )
    tokens_full = lax.all_gather(tokens, "tensor", axis=0, tiled=True)
    group_rows = tokens_full.shape[0]
    member, segment, position, first_rows = row_layout(seq_lengths[0], seq_offsets[0], group_rows)
    firsts = jnp.dot(
        first_rows.T.astype(jnp.bfloat16), tokens_full, preferred_element_type=jnp.float32
    )
    mu_seq = jnp.mean(firsts, axis=1)
    sd_seq = jnp.sqrt(jnp.mean(jnp.square(firsts - mu_seq[:, None]), axis=1) + stat_eps)
    live = jnp.sum(member, axis=1)
    mu_row = jnp.dot(member, mu_seq, precision=highest)
    sd_row = jnp.dot(member, sd_seq, precision=highest) + (1.0 - live)
    centered = (tokens_full.astype(jnp.float32) - mu_row[:, None]) / sd_row[:, None]
    normed_in, scale_in = rms_norm(centered)
    attn_in = (normed_in * gain_in).astype(jnp.bfloat16)
    projected = jnp.dot(attn_in, w_qkv_full, preferred_element_type=jnp.float32)
    cosine, sine = rotary_tables(position)
    q_rot = rotate(projected[:, :head_width], cosine, sine, 1.0).astype(jnp.bfloat16)
    k_rot = rotate(projected[:, head_width : 2 * head_width], cosine, sine, 1.0).astype(
        jnp.bfloat16
    )
    values = projected[:, 2 * head_width :].astype(jnp.bfloat16)
    heads_out, log_sums = attention_forward(q_rot, k_rot, values, segment)
    heads_low = heads_out.astype(jnp.bfloat16)
    attn_own = lax.psum_scatter(
        jnp.dot(heads_low, w_output_full, preferred_element_type=jnp.float32),
        "tensor",
        scatter_dimension=0,
        tiled=True,
    )
    own_start = lax.axis_index("tensor") * own_rows

    def own_part(array):
        return lax.dynamic_slice_in_dim(array, own_start, own_rows, 0)

    centered_own = own_part(centered)
    resid = centered_own + attn_own
    normed_mid, scale_mid = rms_norm(resid)
    mid_low = (normed_mid * gain_mid).astype(jnp.bfloat16)
    mid_full = lax.all_gather(mid_low, "tensor", axis=0, tiled=True)
    pre_act = jnp.dot(mid_full, w_in_full, preferred_element_type=jnp.float32)
    hidden = jax.nn.silu(pre_act).astype(jnp.bfloat16)
    mlp_own = lax.psum_scatter(
        jnp.dot(hidden, w_out_full, preferred_element_type=jnp.float32).astype(jnp.bfloat16),
        "tensor",
        scatter_dimension=0,
        tiled=True,
    ).astype(jnp.float32)
    final = resid + mlp_own
    mu_own = own_part(mu_row)
    sd_own = own_part(sd_row)
    mixed = (mu_own[:, None] + sd_own[:, None] * final).astype(jnp.bfloat16)
    rows_full, columns_full, gains_full = (
        lax.all_gather(row_blocks, "dp", axis=0, tiled=True),
        lax.all_gather(column_blocks, "dp", axis=1, tiled=True),
        lax.all_gather(gain_pair, "dp", axis=1, tiled=True),
    )
    w_qkv_full, w_in_full, w_output_full, w_out_full, gain_in, gain_mid = split_weights(
        rows_full, columns_full, gains_full, head_width
    )
    grad_out = cotangent.astype(jnp.float32)
    final_grad = grad_out * sd_own[:, None]
    mlp_grad_full = lax.all_gather(final_grad.astype(jnp.bfloat16), "tensor", axis=0, tiled=True)
    hidden_grad = against(mlp_grad_full, w_out_full)
    d_w_out = across(hidden, mlp_grad_full)
    sigmoid_act = jax.nn.sigmoid(pre_act)
    act_grad = (hidden_grad * sigmoid_act * (1.0 + pre_act * (1.0 - sigmoid_act))).astype(
        jnp.bfloat16
    )
    d_w_in = across(mid_full, act_grad)
    mid_grad = lax.psum_scatter(
        against(act_grad, w_in_full), "tensor", scatter_dimension=0, tiled=True
    )
    gain_mid_grad = jnp.sum(mid_grad * normed_mid, axis=0)
    resid_grad = final_grad + norm_back(mid_grad * gain_mid, normed_mid, scale_mid)
    attn_grad_full = lax.all_gather(resid_grad.astype(jnp.bfloat16), "tensor", axis=0, tiled=True)
    heads_grad = against(attn_grad_full, w_output_full).astype(jnp.bfloat16)
    d_w_output = across(heads_low, attn_grad_full)
    q_rot_grad, k_rot_grad, values_grad = attention_backward(
        q_rot, k_rot, values, segment, log_sums, heads_grad
    )
    proj_grad = jnp.concatenate(
        [
            rotate(q_rot_grad, cosine, sine, -1.0).astype(jnp.bfloat16),
            rotate(k_rot_grad, cosine, sine, -1.0).astype(jnp.bfloat16),
            values_grad.astype(jnp.bfloat16),
        ],
        axis=1,
    )
    d_w_qkv = across(attn_in, proj_grad)
    in_grad = lax.psum_scatter(
        against(proj_grad, w_qkv_full), "tensor", scatter_dimension=0, tiled=True
    )
    normed_own = own_part(normed_in)
    gain_in_grad = jnp.sum(in_grad * normed_own, axis=0)
    centered_grad = resid_grad + norm_back(in_grad * gain_in, normed_own, own_part(scale_in))
    scaled_grad = centered_grad / sd_own[:, None]
    per_row = jnp.stack(
        [
            jnp.sum(grad_out - scaled_grad, axis=1),
            jnp.sum(grad_out * final - scaled_grad * centered_own, axis=1),
        ],
        axis=1,
    )
    seq_part = jnp.dot(own_part(member).T, per_row, precision=highest)
    gain_part = jnp.stack([gain_in_grad, gain_mid_grad])
    gain_total, seq_total = lax.psum((gain_part, seq_part), "tensor")
    first_own = own_part(first_rows)
    mean_term = jnp.dot(first_own, seq_total[:, 0] / feature_count, precision=highest)
    spread_term = jnp.dot(first_own, seq_total[:, 1] / (feature_count * sd_seq), precision=highest)
    grad_tokens = (
        scaled_grad
        + mean_term[:, None]
        + spread_term[:, None] * (tokens.astype(jnp.float32) - mu_own[:, None])
    )
    grad_rows, grad_columns, gain_grads = (
        lax.psum_scatter(
            jnp.concatenate([d_w_qkv, d_w_in], axis=1), "dp", scatter_dimension=0, tiled=True
        ),
        lax.psum_scatter(
            jnp.concatenate([d_w_output, d_w_out], axis=0), "dp", scatter_dimension=1, tiled=True
        ),
        lax.psum_scatter(gain_total, "dp", scatter_dimension=1, tiled=True),
    )
    return (
        mixed,
        grad_tokens,
        grad_rows[:, :head_width],
        grad_rows[:, head_width : 2 * head_width],
        grad_rows[:, 2 * head_width : qkv_width],
        grad_columns[:head_width],
        grad_rows[:, qkv_width:],
        grad_columns[head_width:],
        gain_grads[0],
        gain_grads[1],
    )


def solution(mesh):
    in_specs = (
        P(("dp", "tensor"), None),
        P("dp", "tensor"),
        P("dp", "tensor"),
        P("dp", "tensor"),
        P("tensor", "dp"),
        P("dp", "tensor"),
        P("tensor", "dp"),
        P("dp"),
        P("dp"),
        P("dp", None),
        P("dp", None),
        P(("dp", "tensor"), None),
    )
    out_specs = (
        P(("dp", "tensor"), None),
        P(("dp", "tensor"), None),
        P("dp", "tensor"),
        P("dp", "tensor"),
        P("dp", "tensor"),
        P("tensor", "dp"),
        P("dp", "tensor"),
        P("tensor", "dp"),
        P("dp"),
        P("dp"),
    )
    return jax.shard_map(local, mesh=mesh, in_specs=in_specs, out_specs=out_specs, check_vma=False)
```

profile of v0, /device:TPU:0, one launch (start us, length us, event | category | flops | bytes accessed | tf_op | source)
XLA Modules:
  0.0 704.9 jit_solution(5537460930866316930)
XLA Ops:
  11.0 23.0 %all-gather = bf16[16,80,2]{1,2,0:T(2,128)(2,1)S(1)} all-gather(bf16[1,80,2]{1,2,0:T(2,128)(2,1)S(1)} %maximum_bitcast_fusion), channel_id=1, replica_groups=mesh['dp'=16,'tensor'=2] {'dp'}, dimensions={0}, use_global_device_ids=true | all-gather | bytes 5440 | tf_op jit(solution)/shard_map/all_gather | solution.py:198
  43.0 59.9 %all-gather.10.cloned.1.call-done = bf16[1280,2560]{1,0:T(8,128)(2,1)} async-done(((bf16[80,2560]{1,0:T(8,128)(2,1)}), bf16[1280,2560]{1,0:T(8,128)(2,1)}) %all-gather.10.cloned.1.call-update) | async-done | bytes 6553616 | tf_op jit(solution)/shard_map/all_gather | solution.py:196
  102.9 5.6 fusion.4
  122.8 27.3 %all-gather.12.cloned.1.call-done = bf16[1280,1280]{0,1:T(8,128)(2,1)} async-done(((bf16[1280,80]{0,1:T(8,128)(2,1)}), bf16[1280,1280]{0,1:T(8,128)(2,1)}) %all-gather.12.cloned.1.call-update) | async-done | bytes 3276816 | tf_op jit(solution)/shard_map/all_gather | solution.py:197
  154.4 36.5 %reduce-scatter.12.cloned.1.call-done = f32[256,1280]{1,0:T(8,128)} async-done(((f32[512,1280]{1,0:T(8,128)}), f32[256,1280]{1,0:T(8,128)}) %reduce-scatter.12.cloned.1.call-update) | async-done | bytes 1310736 | tf_op jit(solution)/shard_map/reduce_scatter | solution.py:226
  195.4 23.0 %all-gather.14.cloned.1.call-done = bf16[512,1280]{1,0:T(8,128)(2,1)} async-done(((bf16[256,1280]{1,0:T(8,128)(2,1)}), bf16[512,1280]{1,0:T(8,128)(2,1)}) %all-gather.14.cloned.1.call-update) | async-done | bytes 1310736 | tf_op jit(solution)/shard_map/all_gather | solution.py:241
  222.5 21.7 %all-gather.16.cloned.1.call-done = bf16[512,1280]{1,0:T(8,128)(2,1)} async-done(((bf16[256,1280]{1,0:T(8,128)(2,1)}), bf16[512,1280]{1,0:T(8,128)(2,1)}) %all-gather.16.cloned.1.call-update) | async-done | bytes 1310736 | tf_op jit(solution)/shard_map/all_gather | solution.py:264
  247.7 4.5 fusion.15
  252.2 37.7 %reduce-scatter.16.cloned.1.call-done = f32[256,1280]{1,0:T(8,128)} async-done(((f32[512,1280]{1,0:T(8,128)}), f32[256,1280]{1,0:T(8,128)}) %reduce-scatter.16.cloned.1.call-update) | async-done | bytes 1310736 | tf_op jit(solution)/shard_map/reduce_scatter | solution.py:272
  293.6 24.3 %all-gather.18.cloned.1.call-done = bf16[512,1280]{1,0:T(8,128)(2,1)} async-done(((bf16[256,1280]{1,0:T(8,128)(2,1)}), bf16[512,1280]{1,0:T(8,128)(2,1)}) %all-gather.18.cloned.1.call-update) | async-done | bytes 1310736 | tf_op jit(solution)/shard_map/all_gather | solution.py:277
  321.2 4.9 fusion.38
  326.2 4.6 multiply_reduce_fusion
  337.0 4.4 fusion.2
  341.5 4.3 convolution_convert_fusion
  346.1 5.2 fusion.81
  354.1 25.1 %reduce-scatter.18.cloned.1.call-done = f32[256,1280]{1,0:T(8,128)} async-done(((f32[512,1280]{1,0:T(8,128)}), f32[256,1280]{1,0:T(8,128)}) %reduce-scatter.18.cloned.1.call-update) | async-done | bytes 1310736 | tf_op jit(solution)/shard_map/reduce_scatter | solution.py:292
  382.5 6.1 pad_maximum_fusion.1
  388.5 8.1 %copy.78 = f32[1280,1280]{0,1:T(8,128)} copy(f32[1280,1280]{1,0:T(8,128)} %pad_maximum_fusion.1) | data formatting | bytes 13107200
  402.7 5.3 pad_maximum_fusion
  408.9 5.0 fusion.41
  414.0 50.3 %reduce-scatter.24.cloned.1.call-done = f32[80,2]{1,0:T(8,128)} async-done(((f32[1280,2]{1,0:T(8,128)}), f32[80,2]{1,0:T(8,128)}) %reduce-scatter.24.cloned.1.call-update) | async-done | bytes 656
  465.2 4.9 all-reduce
  473.7 81.0 %reduce-scatter.22.cloned.1.call-done = f32[80,1280]{1,0:T(8,128)} async-done(((f32[1280,1280]{1,0:T(8,128)}), f32[80,1280]{1,0:T(8,128)}) %reduce-scatter.22.cloned.1.call-update) | async-done | bytes 409616
  556.5 139.7 %reduce-scatter.20.cloned.1.call-done = f32[80,2560]{1,0:T(8,128)} async-done(((f32[1280,2560]{1,0:T(8,128)}), f32[80,2560]{1,0:T(8,128)}) %reduce-scatter.20.cloned.1.call-update) | async-done | bytes 819216 | tf_op jit(solution)/shard_map/reduce_scatter | solution.py:318
  (179 shorter events, 77.8 us)
Async XLA Ops:
  7.2 29.4 %all-gather.8.cloned.1.call-start = ((), (), s32[]{:S(2)}) async-start(), calls=%async_computation.7 | async-start | bytes 1966080 | tf_op jit(solution)/shard_map/all_gather | solution.py:203
  8.0 94.9 %all-gather.10.cloned.1.call-start = ((), (), s32[]{:S(2)}) async-start(), calls=%async_computation.8 | async-start | bytes 6963200 | tf_op jit(solution)/shard_map/all_gather | solution.py:196
  9.9 140.3 %all-gather.12.cloned.1.call-start = ((), (), s32[]{:S(2)}) async-start(), calls=%async_computation.9 | async-start | bytes 3481600 | tf_op jit(solution)/shard_map/all_gather | solution.py:197
  10.7 180.3 %reduce-scatter.12.cloned.1.call-start = ((), (), s32[]{:S(2)}) async-start(), calls=%async_computation.10 | async-start | bytes 3932160 | tf_op jit(solution)/shard_map/reduce_scatter | solution.py:226
  10.8 28.3 %copy-start.28 = (s32[5]{0:T(128)}, s32[5]{0:T(128)S(1)}, u32[]{:S(2)}) copy-start(s32[5]{0:T(128)S(1)} %add_bitcast_fusion) | copy-start | bytes 64
  112.4 6.8 copy-start.9
  122.8 31.5 %copy-start.21 = (bf16[8,80,512]{2,1,0:T(8,128)(2,1)}, bf16[8,80,512]{2,1,0:T(8,128)(2,1)S(1)}, u32[]{:S(2)}) copy-start(bf16[8,80,512]{2,1,0:T(8,128)(2,1)S(1)} %fusion.37) | copy-start | bytes 1966084
  154.4 64.0 %all-gather.14.cloned.1.call-start = ((), (), s32[]{:S(2)}) async-start(), calls=%async_computation.11 | async-start | bytes 1966080 | tf_op jit(solution)/shard_map/all_gather | solution.py:241
  194.0 50.2 %all-gather.16.cloned.1.call-start = ((), (), s32[]{:S(2)}) async-start(), calls=%async_computation.13 | async-start | bytes 1966080 | tf_op jit(solution)/shard_map/all_gather | solution.py:264
  195.2 94.7 %reduce-scatter.16.cloned.1.call-start = ((), (), s32[]{:S(2)}) async-start(), calls=%async_computation.14 | async-start | bytes 3932160 | tf_op jit(solution)/shard_map/reduce_scatter | solution.py:272
  247.7 4.5 copy-start.23
  252.2 65.8 %all-gather.18.cloned.1.call-start = ((), (), s32[]{:S(2)}) async-start(), calls=%async_computation.15 | async-start | bytes 1966080 | tf_op jit(solution)/shard_map/all_gather | solution.py:277
  293.5 85.7 %reduce-scatter.18.cloned.1.call-start = ((), (), s32[]{:S(2)}) async-start(), calls=%async_computation.16 | async-start | bytes 3932160 | tf_op jit(solution)/shard_map/reduce_scatter | solution.py:292
  321.2 5.0 copy-start.10
  321.2 9.6 %slice-start = ((s8[8388608]{0:T(1024)(128)(4,1)}), s8[4194304]{0:T(1024)(128)(4,1)S(1)}, s32[]{:S(2)}) async-start(s8[8388608]{0:T(1024)(128)(4,1)} %bitcast.74), calls=%async_computation.20 | async-start | bytes 8388608
  326.2 4.7 slice-start.1
  341.5 67.4 %reduce-scatter.14.cloned.1.call-start = ((), (), s32[]{:S(2)}) async-start(), calls=%async_computation.12 | async-start | bytes 1966080 | tf_op jit(solution)/shard_map/reduce_scatter | solution.py:244
  345.8 118.5 %reduce-scatter.24.cloned.1.call-start = ((), (), s32[]{:S(2)}) async-start(), calls=%async_computation.19 | async-start | bytes 696320
  346.1 5.2 copy-start.20
  346.1 5.2 copy-start.22
  382.4 172.3 %reduce-scatter.22.cloned.1.call-start = ((), (), s32[]{:S(2)}) async-start(), calls=%async_computation.18 | async-start | bytes 6963200
  396.7 299.5 %reduce-scatter.20.cloned.1.call-start = ((), (), s32[]{:S(2)}) async-start(), calls=%async_computation.17 | async-start | bytes 13926400 | tf_op jit(solution)/shard_map/reduce_scatter | solution.py:318
  408.9 61.9 %copy-start.31 = (f32[5]{0:T(128)S(1)}, f32[5]{0:T(128)}, u32[]{:S(2)}) copy-start(f32[5]{0:T(128)} %copy-done.30) | copy-start | bytes 64
  408.9 62.1 %copy-start.11 = (bf16[256,1280]{1,0:T(8,128)(2,1)S(1)}, bf16[256,1280]{1,0:T(8,128)(2,1)}, u32[]{:S(2)}) copy-start(bf16[256,1280]{1,0:T(8,128)(2,1)} %param.12) | copy-start | bytes 1966084
  (28 other events, 62.7 us)
Sparse Core Ops, SparseCore 0:
  9.6 26.9 all-gather.7
  39.5 63.3 all-gather.9
  105.7 44.3 all-gather.11
  154.5 36.4 reduce-scatter.11
  194.1 24.2 all-gather.13
  219.9 24.2 all-gather.15
  252.3 37.5 reduce-scatter.15
  293.6 24.2 all-gather.17
  341.6 37.5 reduce-scatter.17
  381.4 23.1 reduce-scatter.13
  408.2 56.1 reduce-scatter.23
  468.6 85.9 reduce-scatter.21
  558.8 137.3 reduce-scatter.19
where the time goes:
time: 706 us; the launch traced here: 705 us
  waiting for transfers between devices  529 us (75%)
  matrix products  65.1 us (9%)
  other arithmetic  41.5 us (6%)
  blocking collectives  27.9 us (4%)
  local copies, waits for them, and re-layouts  26.3 us (4%)
  between operations  14.6 us (2%)
    reduce_scatter x1, waiting for transfers between devices, local(): lax.psum_scatter(jnp.concatenate([d_w_qkv, d_w_in], axis=1), 'dp', scatte...  140 us
    unnamed x15, waiting for transfers between devices  132 us
    all_gather x1, waiting for transfers between devices, local(): lax.all_gather(row_blocks, 'dp', axis=0, tiled=True)  59.9 us
    reduce_scatter x1, waiting for transfers between devices, local(): lax.psum_scatter(against(act_grad, w_in_full), 'tensor', scatter_dimensio...  37.7 us
    reduce_scatter x1, waiting for transfers between devices, local(): lax.psum_scatter(jnp.dot(heads_low, w_output_full, preferred_element_type...  36.5 us
    all_gather x1, waiting for transfers between devices, local(): lax.all_gather(column_blocks, 'dp', axis=1, tiled=True)  27.3 us
    reduce_scatter x1, waiting for transfers between devices, local(): lax.psum_scatter(against(proj_grad, w_qkv_full), 'tensor', scatter_dimens...  25.1 us
    all_gather x1, waiting for transfers between devices, local(): lax.all_gather(resid_grad.astype(jnp.bfloat16), 'tensor', axis=0, tiled=T...  24.3 us
  transfers between devices with their start and end apart: 13, of which 12 were waited for; matrix products, arithmetic and copies ran while one was open for 12% of the time, Pallas kernels for 0%

commit v1 on v0

--- a/solution.py
+++ b/solution.py
@@ -1,6 +1,9 @@
 import jax
 import jax.numpy as jnp
 from jax import lax
+from jax.experimental import pallas as pl
+from jax.experimental.pallas import tpu as pltpu
+from jax.sharding import Mesh
 from jax.sharding import PartitionSpec as P
 
 HEAD_DIM = 80
@@ -337,7 +340,302 @@
     )
 
 
+ALL_AXES = ("z", "x", "c", "y")
+
+
+def flip(value, axis):
+    return lax.ppermute(value, axis, [(0, 1), (1, 0)])
+
+
+def shift_z(value, step):
+    return lax.ppermute(value, "z", [(i, (i + step) % 4) for i in range(4)])
+
+
+def flip_split(value, first):
+    pairs = []
+    for z in range(4):
+        for x in range(2):
+            for c in range(2):
+                for y in range(2):
+                    there = (z, 1 - x, c, y) if c == first else (z, x, c, 1 - y)
+                    here = ((z * 2 + x) * 2 + c) * 2 + y
+                    pairs.append((here, ((there[0] * 2 + there[1]) * 2 + there[2]) * 2 + there[3]))
+    return lax.ppermute(value, ALL_AXES, pairs)
+
+
+def assemble_rows(place, blocks):
+    count = len(blocks)
+    width = blocks[0].shape[1]
+
+    def body(place_ref, *refs):
+        ins, (full, tail) = refs[:count], refs[count:]
+        for i, block in enumerate(ins):
+            spot = place_ref[i]
+            row = pl.multiple_of(spot * 80, 16)
+            for j in range(3):
+                full[pl.ds(row, 80), pl.ds(width * j, width)] = block[pl.ds(80 * j, 80), :]
+            tail[spot] = block[pl.ds(240, 16), :]
+
+    return pl.pallas_call(
+        body,
+        out_shape=(
+            jax.ShapeDtypeStruct((1280, 3 * width), jnp.bfloat16),
+            jax.ShapeDtypeStruct((16, 16, width), jnp.bfloat16),
+        ),
+        in_specs=[pl.BlockSpec(memory_space=pltpu.SMEM)]
+        + [pl.BlockSpec(memory_space=pltpu.VMEM)] * count,
+        out_specs=(pl.BlockSpec(memory_space=pltpu.VMEM),) * 2,
+        compiler_params=pltpu.CompilerParams(vmem_limit_bytes=24 * 2**20),
+        name="assemble_rows",
+    )(place, *blocks)
+
+
+def assemble_pairs(place, half, blocks):
+    count = len(blocks)
+    width = blocks[0].shape[1]
+
+    def body(place_ref, half_ref, *refs):
+        ins, outs = refs[:count], refs[count:]
+        for i, block in enumerate(ins):
+            row = pl.multiple_of(place_ref[i] * 80, 16)
+            for j in range(3):
+                outs[j][half_ref[i], pl.ds(row, 80), :] = block[pl.ds(80 * j, 80), :]
+
+    return pl.pallas_call(
+        body,
+        out_shape=(jax.ShapeDtypeStruct((2, 1280, width), jnp.bfloat16),) * 3,
+        in_specs=[pl.BlockSpec(memory_space=pltpu.SMEM)] * 2
+        + [pl.BlockSpec(memory_space=pltpu.VMEM)] * count,
+        out_specs=(pl.BlockSpec(memory_space=pltpu.VMEM),) * 3,
+        compiler_params=pltpu.CompilerParams(vmem_limit_bytes=40 * 2**20),
+        name="assemble_pairs",
+    )(place, half, *blocks)
+
+
+def pick(array, index, axis):
+    return lax.dynamic_index_in_dim(array, index, axis, keepdims=False)
+
+
+def low16(value):
+    return value.astype(jnp.bfloat16)
+
+
+def wide(value):
+    return value.astype(jnp.float32)
+
+
+def local_fast(
+    tokens,
+    w_query,
+    w_key,
+    w_value,
+    w_output,
+    w_in,
+    w_out,
+    gain_attn,
+    gain_mlp,
+    seq_lengths,
+    seq_offsets,
+    cotangent,
+):
+    z, x, c, y = (lax.axis_index(name) for name in ALL_AXES)
+    own_rows, feature_count = tokens.shape
+    head_width = w_query.shape[1]
+
+    gains = jnp.pad(
+        jnp.stack([gain_attn, gain_mlp]), ((0, 14), (0, head_width - gain_attn.shape[0]))
+    )
+    q_block = jnp.concatenate([w_query, w_key, w_value, gains], axis=0)
+    p_block = jnp.concatenate([w_output.T, w_in, w_out.T], axis=0)
+    tokens_other = flip(tokens, "y")
+    q_z = [q_block] + [shift_z(q_block, step) for step in (1, 3, 2)]
+    q_mine = q_z + [flip(block, "x") for block in q_z]
+    q_other = [flip(block, "c") for block in q_mine]
+    steps = (0, 1, 3, 2)
+    q_place = jnp.stack(
+        [
+            ((z - step) % 4 * 2 + (x ^ xr)) * 2 + (c ^ cr)
+            for cr in range(2)
+            for xr in range(2)
+            for step in steps
+        ]
+    ).astype(jnp.int32)
+    w_qkv_full, tails = assemble_rows(q_place, q_mine + q_other)
+    gain_in = wide(tails[:, 0, :80].reshape(-1))
+    gain_mid = wide(tails[:, 1, :80].reshape(-1))
+
+    p_z = [p_block] + [shift_z(p_block, step) for step in (1, 3, 2)]
+    p_second = [flip_split(block, 0) for block in p_z]
+    p_third = [flip_split(block, 1) for block in p_z + p_second]
+    p_mine = p_z + p_second + p_third
+    p_other = [flip(block, "c") for block in p_mine]
+    places, halves = [], []
+    for cr in range(2):
+        side = c ^ cr
+        for third in range(2):
+            for second in range(2):
+                xr = jnp.where(side == 0, second, third)
+                yr = jnp.where(side == 0, third, second)
+                for step in steps:
+                    places.append(((z - step) % 4 * 2 + (x ^ xr)) * 2 + side)
+                    halves.append(yr)
+    wo, wi, wt = assemble_pairs(
+        jnp.stack(places).astype(jnp.int32), jnp.stack(halves).astype(jnp.int32), p_mine + p_other
+    )
+
+    def both(own, other):
+        return jnp.where(
+            y == 0, jnp.concatenate([own, other], 0), jnp.concatenate([other, own], 0)
+        )
+
+    def own_part(array):
+        return lax.dynamic_slice_in_dim(array, y * own_rows, own_rows, 0)
+
+    def other_part(array):
+        return lax.dynamic_slice_in_dim(array, (1 - y) * own_rows, own_rows, 0)
+
+    tokens_full = both(tokens, tokens_other)
+    group_rows = tokens_full.shape[0]
+    member, segment, position, first_rows = row_layout(seq_lengths[0], seq_offsets[0], group_rows)
+    firsts = jnp.dot(first_rows.T.astype(jnp.bfloat16), tokens_full, preferred_element_type=jnp.float32)
+    mu_seq = jnp.mean(firsts, axis=1)
+    sd_seq = jnp.sqrt(jnp.mean(jnp.square(firsts - mu_seq[:, None]), axis=1) + stat_eps)
+    live = jnp.sum(member, axis=1)
+    mu_row = jnp.dot(member, mu_seq, precision=highest)
+    sd_row = jnp.dot(member, sd_seq, precision=highest) + (1.0 - live)
+    centered = (wide(tokens_full) - mu_row[:, None]) / sd_row[:, None]
+    normed_in, scale_in = rms_norm(centered)
+    attn_in = low16(normed_in * gain_in)
+    projected = jnp.dot(attn_in, w_qkv_full, preferred_element_type=jnp.float32)
+    cosine, sine = rotary_tables(position)
+    q_rot = low16(rotate(projected[:, :head_width], cosine, sine, 1.0))
+    k_rot = low16(rotate(projected[:, head_width : 2 * head_width], cosine, sine, 1.0))
+    values = low16(projected[:, 2 * head_width :])
+    heads_out, log_sums = attention_forward(q_rot, k_rot, values, segment)
+    heads_low = low16(heads_out)
+    heads = [own_part(heads_low), flip(other_part(heads_low), "y")]
+    attn_own = against(heads[0], wo[0]) + against(heads[1], wo[1])
+    centered_own = own_part(centered)
+    resid = centered_own + attn_own
+    normed_mid, scale_mid = rms_norm(resid)
+    mid_low = low16(normed_mid * gain_mid)
+    pre_act = [jnp.dot(mid_low, wi[r], preferred_element_type=jnp.float32) for r in range(2)]
+    hidden = [low16(jax.nn.silu(part)) for part in pre_act]
+    final = resid + against(hidden[0], wt[0]) + against(hidden[1], wt[1])
+    mu_own, sd_own = own_part(mu_row), own_part(sd_row)
+    mixed = low16(mu_own[:, None] + sd_own[:, None] * final)
+
+    grad_out = wide(cotangent)
+    final_grad = grad_out * sd_own[:, None]
+    mlp_grad = low16(final_grad)
+    act_grad = []
+    for r in range(2):
+        hidden_grad = jnp.dot(mlp_grad, wt[r], preferred_element_type=jnp.float32)
+        sigmoid_act = jax.nn.sigmoid(pre_act[r])
+        act_grad.append(
+            low16(hidden_grad * sigmoid_act * (1.0 + pre_act[r] * (1.0 - sigmoid_act)))
+        )
+    mid_grad = against(act_grad[0], wi[0]) + against(act_grad[1], wi[1])
+    gain_mid_grad = jnp.sum(mid_grad * normed_mid, axis=0)
+    resid_grad = final_grad + norm_back(mid_grad * gain_mid, normed_mid, scale_mid)
+    attn_grad = low16(resid_grad)
+    heads_grad = [
+        low16(jnp.dot(attn_grad, wo[r], preferred_element_type=jnp.float32)) for r in range(2)
+    ]
+    heads_grad_full = both(heads_grad[0], flip(heads_grad[1], "y"))
+
+    def chunks(array):
+        return array.reshape(4, 2, 2, 80, array.shape[-1])
+
+    def core_sum(array):
+        parts = chunks(array)
+        return pick(parts, c, 2) + wide(flip(low16(pick(parts, 1 - c, 2)), "c"))
+
+    def x_sum(array):
+        return pick(array, x, 1) + wide(flip(low16(pick(array, 1 - x, 1)), "x"))
+
+    def z_sum(array):
+        total = pick(array, z, 0)
+        for step in (1, 3, 2):
+            total = total + wide(shift_z(low16(pick(array, (z + step) % 4, 0)), step))
+        return total
+
+    d_wt = [core_sum(across(mlp_grad, hidden[r])) for r in range(2)]
+    d_wi = [core_sum(across(mid_low, act_grad[r])) for r in range(2)]
+    d_wo = [core_sum(across(attn_grad, heads[r])) for r in range(2)]
+    d_wt = x_sum(d_wt[0] + wide(flip(low16(d_wt[1]), "y")))
+    d_wi_x = [x_sum(part) for part in d_wi]
+    d_wi = d_wi_x[0] + wide(flip(low16(d_wi_x[1]), "y"))
+    d_wo = x_sum(d_wo[0] + wide(flip(low16(d_wo[1]), "y")))
+    d_p = z_sum(jnp.concatenate([d_wo, d_wi, d_wt], axis=1))
+
+    q_rot_grad, k_rot_grad, values_grad = attention_backward(
+        q_rot, k_rot, values, segment, log_sums, heads_grad_full
+    )
+    proj_grad = jnp.concatenate(
+        [
+            low16(rotate(q_rot_grad, cosine, sine, -1.0)),
+            low16(rotate(k_rot_grad, cosine, sine, -1.0)),
+            low16(values_grad),
+        ],
+        axis=1,
+    )
+    in_grad_all = against(proj_grad, w_qkv_full)
+    in_grad = own_part(in_grad_all) + wide(flip(low16(other_part(in_grad_all)), "y"))
+    gain_in_grad = jnp.sum(in_grad_all * normed_in, axis=0)
+    d_qkv = z_sum(x_sum(core_sum(across(attn_in, proj_grad))))
+    normed_own = own_part(normed_in)
+    centered_grad = resid_grad + norm_back(in_grad * gain_in, normed_own, own_part(scale_in))
+    scaled_grad = centered_grad / sd_own[:, None]
+    per_row = jnp.stack(
+        [
+            jnp.sum(grad_out - scaled_grad, axis=1),
+            jnp.sum(grad_out * final - scaled_grad * centered_own, axis=1),
+        ],
+        axis=1,
+    )
+    seq_part = jnp.dot(own_part(member).T, per_row, precision=highest)
+    seq_total = seq_part + flip(seq_part, "y")
+    first_own = own_part(first_rows)
+    mean_term = jnp.dot(first_own, seq_total[:, 0] / feature_count, precision=highest)
+    spread_term = jnp.dot(first_own, seq_total[:, 1] / (feature_count * sd_seq), precision=highest)
+    grad_tokens = (
+        scaled_grad
+        + mean_term[:, None]
+        + spread_term[:, None] * (wide(tokens) - mu_own[:, None])
+    )
+    gain_total = lax.psum(jnp.stack([gain_in_grad, gain_mid_grad]), ALL_AXES)
+    place = (z * 2 + x) * 2 + c
+    gain_grads = lax.dynamic_slice_in_dim(gain_total, place * 80, 80, 1)
+    return (
+        mixed,
+        grad_tokens,
+        d_qkv[:, :head_width],
+        d_qkv[:, head_width : 2 * head_width],
+        d_qkv[:, 2 * head_width :],
+        d_p[:80].T,
+        d_p[80:160],
+        d_p[160:].T,
+        gain_grads[0],
+        gain_grads[1],
+    )
+
+
+def solution_fast(mesh):
+    fine = Mesh(mesh.devices.reshape(4, 2, 2, 2), ALL_AXES)
+    dp = ("z", "x", "c")
+    rows, by_row, by_column = P(ALL_AXES, None), P(dp, "y"), P("y", dp)
+    in_specs = (rows,) + (by_row,) * 3 + (by_column, by_row, by_column)
+    in_specs += (P(dp), P(dp), P(dp, None), P(dp, None), rows)
+    out_specs = (rows, rows) + (by_row,) * 3 + (by_column, by_row, by_column, P(dp), P(dp))
+    return jax.shard_map(
+        local_fast, mesh=fine, in_specs=in_specs, out_specs=out_specs, check_vma=False
+    )
+
+
 def solution(mesh):
+    if dict(mesh.shape) == {"dp": 16, "tensor": 2}:
+        return solution_fast(mesh)
     in_specs = (
         P(("dp", "tensor"), None),
         P("dp", "tensor"),

time: 706 us -> 416 us (0.59)
  waiting for transfers between devices: 529 us -> 146 us
  starting transfers between devices: 0.94 us -> 79.4 us
  local copies, waits for them, and re-layouts: 26.3 us -> 49.8 us
  blocking collectives: 27.9 us -> 46.2 us
  matrix products: 65.1 us -> 50.8 us
  between operations: 14.6 us -> 2.13 us
  other arithmetic: 41.5 us -> 29.2 us
    reduce_scatter x5 -> x0, waiting for transfers between devices: 239 us -> none  [the longest x1 140 us: local(): lax.psum_scatter(jnp.concatenate([d_w_qkv, d_w_in], axis=1), 'dp', scatte...]
    all_gather x6 -> x0, waiting for transfers between devices: 157 us -> none  [the longest x1 59.9 us: local(): lax.all_gather(row_blocks, 'dp', axis=0, tiled=True)]
    ppermute x0 -> x72, waiting for transfers between devices: none -> 146 us  [the longest x48 87 us: flip(): return lax.ppermute(value, axis, [(0, 1), (1, 0)])]
    unnamed x15 -> x0, waiting for transfers between devices: 132 us -> none
    ppermute x0 -> x72, starting transfers between devices: none -> 79.4 us  [the longest x12 37.1 us: shift_z(): return lax.ppermute(value, 'z', [(i, (i + step) % 4) for i in range(4)])]
    psum x1, blocking collectives: 4.93 us -> 46.2 us  [local_fast(): gain_total = lax.psum(jnp.stack([gain_in_grad, gain_mid_grad]), ALL_AXES)]
    all_gather x1 -> x0, blocking collectives: 23 us -> none  [local(): lax.all_gather(gain_pair, 'dp', axis=1, tiled=True)]
    concatenate x4 -> x3, other arithmetic: 13.9 us -> 2.21 us  [the longest x1 1.03 us: local_fast(): q_block = jnp.concatenate([w_query, w_key, w_value, gains], axis=0)]
  transfers between devices with their start and end apart: 13 -> 72, of which waited for: 12 -> 19; matrix products, arithmetic and copies ran while one was open for 12% -> 21% of each run, Pallas kernels for 0% -> 2%
where the time goes in v1:
time: 416 us; the launch traced here: 410 us
  waiting for transfers between devices  146 us (35%)
  starting transfers between devices  79.4 us (19%)
  matrix products  50.8 us (12%)
  local copies, waits for them, and re-layouts  49.8 us (12%)
  blocking collectives  46.2 us (11%)
  other arithmetic  29.2 us (7%)
  Pallas kernels  6.19 us (1%)
    ppermute x48, waiting for transfers between devices, flip(): return lax.ppermute(value, axis, [(0, 1), (1, 0)])  87 us
    ppermute x12, waiting for transfers between devices, shift_z(): return lax.ppermute(value, 'z', [(i, (i + step) % 4) for i in range(4)])  50 us
    psum x1, blocking collectives, local_fast(): gain_total = lax.psum(jnp.stack([gain_in_grad, gain_mid_grad]), ALL_AXES)  46.2 us
    ppermute x12, starting transfers between devices, shift_z(): return lax.ppermute(value, 'z', [(i, (i + step) % 4) for i in range(4)])  37.1 us
    ppermute x48, starting transfers between devices, flip(): return lax.ppermute(value, axis, [(0, 1), (1, 0)])  29 us
    unnamed x178, local copies, waits for them, and re-layouts  24.4 us
    dot_general x7, matrix products, against(): lax.dot_general(left, right, contract_last, preferred_element_type=jnp.fl...  16.3 us
    ppermute x12, starting transfers between devices, flip_split(): return lax.ppermute(value, ALL_AXES, pairs)  13.4 us
  transfers between devices with their start and end apart: 72, of which 19 were waited for; matrix products, arithmetic and copies ran while one was open for 21% of the time, Pallas kernels for 2%

profile of v1, /device:TPU:0, one launch (start us, length us, event | category | flops | bytes accessed | tf_op | source)
XLA Modules:
  0.0 410.2 jit_solution(11564238472421804031)
XLA Ops:
  16.3 5.4 %collective-permute-done.2.refs_2_ = bf16[256,640]{1,0:T(8,128)(2,1)S(1)} collective-permute-done((bf16[256,640]{1,0:T(8,128)(2,1)S(1)}, bf16[256,640]{1,0:T(8,128)(2,1)S(1)}, u32[]{:S(2)}, u32[]{:S(2)}) %collective-permute-start.2) | collective-permute-done | bytes 327712 | tf_op jit(solution)/shard_map/ppermute | solution.py:351
  27.3 9.0 %collective-permute-done.3.refs_3_ = bf16[256,640]{1,0:T(8,128)(2,1)S(1)} collective-permute-done((bf16[256,640]{1,0:T(8,128)(2,1)S(1)}, bf16[256,640]{1,0:T(8,128)(2,1)S(1)}, u32[]{:S(2)}, u32[]{:S(2)}) %collective-permute-start.3) | collective-permute-done | bytes 327712 | tf_op jit(solution)/shard_map/ppermute | solution.py:351
  39.3 7.1 %collective-permute-done.7.refs_7_ = bf16[256,640]{1,0:T(8,128)(2,1)S(1)} collective-permute-done((bf16[256,640]{1,0:T(8,128)(2,1)S(1)}, bf16[256,640]{1,0:T(8,128)(2,1)S(1)}, u32[]{:S(2)}, u32[]{:S(2)}) %collective-permute-start.7) | collective-permute-done | bytes 327712 | tf_op jit(solution)/shard_map/ppermute | solution.py:347
  46.5 7.0 %collective-permute-start.16 = (bf16[240,640]{1,0:T(8,128)(2,1)S(1)}, bf16[240,640]{1,0:T(8,128)(2,1)S(1)}, u32[]{:S(2)}, u32[]{:S(2)}) collective-permute-start(bf16[240,640]{1,0:T(8,128)(2,1)S(1)} %pad_maximum_fusion.13.refs_0_), channel_id=1, source_target_pairs={{0,8},{8,16},{16,24},{24,0},{1,9},{9,17},{17,25},{25,1},{2,10},{10... | collective-permute-start | bytes 921608 | tf_op jit(solution)/shard_map/ppermute | solution.py:351
  55.9 3.9 collective-permute-start.18
  69.3 5.8 %fusion.97 = f32[512,1920]{1,0:T(8,128)S(1)} fusion(bf16[1280,1920]{1,0:T(8,128)(2,1)} %copy-done.22, f32[512,1280]{1,0:T(8,128)} %broadcast_multiply_fusion, f32[1280]{0:T(1024)S(1)} %reshape.360), kind=kOutput, calls=%fused_computation.163 | convolution fusion | flops 2517893120 | bytes 11473920 | tf_op jit(solution)/shard_map/dot_general | solution.py:509
  99.3 3.6 collective-permute-done.27.refs_12_
  136.8 5.2 %assemble_pairs.1 = (bf16[2,1280,640]{2,1,0:T(8,128)(2,1)S(1)}, bf16[2,1280,640]{2,1,0:T(8,128)(2,1)}, bf16[2,1280,640]{2,1,0:T(8,128)(2,1)}) custom-call(s32[32]{0:T(128)S(1)} %stack.224.place_ref, s32[32]{0:T(128)S(1)} %stack.229.half_ref, bf16[240,640]{1,0:T(8,128)(2,1)S(1)} %pad_maximum_fusion.13.refs_0_, ...), custom_call_target="tpu_custom_call" | custom-call | tf_op jit(solution)/shard_map/assemble_pairs/pallas_call | solution.py:404
  172.5 4.7 %collective-permute-done.48 = bf16[256,640]{1,0:T(8,128)(2,1)S(1)} collective-permute-done((bf16[256,640]{1,0:T(8,128)(2,1)S(1)}, bf16[256,640]{1,0:T(8,128)(2,1)S(1)}, u32[]{:S(2)}, u32[]{:S(2)}) %collective-permute-start.48) | collective-permute-done | bytes 327712 | tf_op jit(solution)/shard_map/ppermute | solution.py:347
  177.4 5.2 %multiply_reduce_fusion = (f32[8,512]{1,0:T(8,128)S(1)}, f32[8,512,512]{1,2,0:T(8,128)S(1)}) fusion(f32[8,512,512]{1,2,0:T(8,128)} %copy-done.23, f32[8,512]{1,0:T(8,128)S(1)} %log_add_fusion, bf16[512,8,80]{0,2,1:T(8,128)(2,1)S(1)} %bitcast.281, bf16[256,8,80]{0,2,1:T(8,128)(2,1)S(1)} %bitcast.272, bf16[256,8,80]{0,2,1:T(8,128)(2,1)S(1)} %bitcast.270, ...), kind=kOutput, calls=%fused_computation.1 | convolution fusion | flops 344780800 | bytes 18120704 | tf_op jit(solution)/shard_map/while/body/eval_jaxpr/qhd,khd->hqk/dot_general | solution.py:132
  192.0 4.5 %multiply_reduce_fusion.1 = (f32[1280]{0:T(1024)S(1)}, f32[512,1280]{1,0:T(8,128)}) fusion(f32[512,1280]{1,0:T(8,128)S(1)} %copy-done.24, bf16[1280,1920]{1,0:T(8,128)(2,1)S(1)} %bitcast.253, bf16[512,640]{0,1:T(8,128)(2,1)S(1)} %bitcast.274, bf16[512,640]{0,1:T(8,128)(2,1)S(1)} %bitcast.278, bf16[512,640]{0,1:T(8,128)(2,1)S(1)} %bitcast.276), kind=kOutput, calls=%fused_computation.18 | convolution fusion | flops 2523790080 | bytes 12129280 | tf_op jit(solution)/shard_map/dot_general | solution.py:21
  196.6 5.4 %fusion.91 = f32[1280,1920]{1,0:T(8,128)} fusion(bf16[512,640]{0,1:T(8,128)(2,1)S(1)} %bitcast.275, bf16[512,640]{0,1:T(8,128)(2,1)S(1)} %bitcast.279, bf16[512,640]{0,1:T(8,128)(2,1)S(1)} %bitcast.277, f32[512,1280]{1,0:T(8,128)S(1)} %copy-done.24, f32[1280]{0:T(1024)S(1)} %copy-done.64), kind=kOutput, calls=%fused_computation.132 | convolution fusion | flops 2523791360 | bytes 14423040 | tf_op jit(solution)/shard_map/dot_general | solution.py:25
  202.0 46.2 %psum.7 = f32[2,1280]{1,0:T(2,128)S(1)} all-reduce(f32[2,1280]{1,0:T(2,128)S(1)} %pad_maximum_fusion.14), channel_id=1, replica_groups=mesh['z'=4,'x'=2,'c'=2,'y'=2] {'z','x','c','y'}, use_global_device_ids=true, to_apply=%region_16.17 | all-reduce | flops 2560 | bytes 20480 | tf_op jit(solution)/shard_map/psum | solution.py:607
  262.9 9.7 %collective-permute-done.49 = bf16[256,1280]{1,0:T(8,128)(2,1)S(1)} collective-permute-done((bf16[256,1280]{1,0:T(8,128)(2,1)S(1)}, bf16[256,1280]{1,0:T(8,128)(2,1)S(1)}, u32[]{:S(2)}, u32[]{:S(2)}) %collective-permute-start.49) | collective-permute-done | bytes 655392 | tf_op jit(solution)/shard_map/ppermute | solution.py:347
  273.1 4.0 fusion.52
  279.2 10.6 %collective-permute-done.50 = f32[5,2]{0,1:T(2,128)S(1)} collective-permute-done((f32[5,2]{0,1:T(2,128)S(1)}, f32[5,2]{0,1:T(2,128)S(1)}, u32[]{:S(2)}, u32[]{:S(2)}) %collective-permute-start.50) | collective-permute-done | bytes 72 | tf_op jit(solution)/shard_map/ppermute | solution.py:347
  293.3 7.5 %collective-permute-done.63 = bf16[4,80,640]{2,1,0:T(8,128)(2,1)S(1)} collective-permute-done((bf16[4,80,640]{2,1,0:T(8,128)(2,1)S(1)}, bf16[4,80,640]{2,1,0:T(8,128)(2,1)S(1)}, u32[]{:S(2)}, u32[]{:S(2)}) %collective-permute-start.63) | collective-permute-done | bytes 409632 | tf_op jit(solution)/shard_map/ppermute | solution.py:347
  308.6 14.9 %collective-permute-done.67 = bf16[4,2,80,640]{3,2,0,1:T(8,128)(2,1)S(1)} collective-permute-done((bf16[4,2,80,640]{3,2,0,1:T(8,128)(2,1)S(1)}, bf16[4,2,80,640]{3,2,0,1:T(8,128)(2,1)S(1)}, u32[]{:S(2)}, u32[]{:S(2)}) %collective-permute-start.67) | collective-permute-done | bytes 819232 | tf_op jit(solution)/shard_map/ppermute | solution.py:347
  324.5 4.8 %collective-permute-done.64 = bf16[4,80,640]{2,1,0:T(8,128)(2,1)S(1)} collective-permute-done((bf16[4,80,640]{2,1,0:T(8,128)(2,1)S(1)}, bf16[4,80,640]{2,1,0:T(8,128)(2,1)S(1)}, u32[]{:S(2)}, u32[]{:S(2)}) %collective-permute-start.64) | collective-permute-done | bytes 409632 | tf_op jit(solution)/shard_map/ppermute | solution.py:347
  329.6 25.2 %collective-permute-done.68 = bf16[4,80,640]{2,1,0:T(8,128)(2,1)S(1)} collective-permute-done((bf16[4,80,640]{2,1,0:T(8,128)(2,1)S(1)}, bf16[4,80,640]{2,1,0:T(8,128)(2,1)S(1)}, u32[]{:S(2)}, u32[]{:S(2)}) %collective-permute-start.68) | collective-permute-done | bytes 409632 | tf_op jit(solution)/shard_map/ppermute | solution.py:347
  363.2 4.0 collective-permute-done.69
  367.2 12.3 %collective-permute-start.55 = (bf16[80,1920]{1,0:T(8,128)(2,1)S(1)}, bf16[80,1920]{1,0:T(8,128)(2,1)S(1)}, u32[]{:S(2)}, u32[]{:S(2)}) collective-permute-start(bf16[80,1920]{1,0:T(8,128)(2,1)S(1)} %get-tuple-element.92), channel_id=1, source_target_pairs={{0,16},{8,24},{16,0},{24,8},{1,17},{9,25},{17,1},{25,9},{2,18},{10... | collective-permute-start | bytes 921608 | tf_op jit(solution)/shard_map/ppermute | solution.py:351
  379.5 17.5 %collective-permute-done.71 = bf16[240,640]{1,0:T(8,128)(2,1)S(1)} collective-permute-done((bf16[240,640]{1,0:T(8,128)(2,1)S(1)}, bf16[240,640]{1,0:T(8,128)(2,1)S(1)}, u32[]{:S(2)}, u32[]{:S(2)}) %collective-permute-start.71) | collective-permute-done | bytes 307232 | tf_op jit(solution)/shard_map/ppermute | solution.py:351
  398.0 11.0 %collective-permute-done.55 = bf16[80,1920]{1,0:T(8,128)(2,1)S(1)} collective-permute-done((bf16[80,1920]{1,0:T(8,128)(2,1)S(1)}, bf16[80,1920]{1,0:T(8,128)(2,1)S(1)}, u32[]{:S(2)}, u32[]{:S(2)}) %collective-permute-start.55) | collective-permute-done | bytes 307232 | tf_op jit(solution)/shard_map/ppermute | solution.py:351
  (423 shorter events, 173.5 us)
Async XLA Ops:
  7.6 28.7 %collective-permute-start.3 = (bf16[256,640]{1,0:T(8,128)(2,1)S(1)}, bf16[256,640]{1,0:T(8,128)(2,1)S(1)}, u32[]{:S(2)}, u32[]{:S(2)}) collective-permute-start(bf16[256,640]{1,0:T(8,128)(2,1)S(1)} %pad_maximum_fusion.12.refs_0_), channel_id=1, source_target_pairs={{0,16},{8,24},{16,0},{24,8},{1,17},{9,25},{17,1},{25,9},{2,18},{10... | collective-permute-start | bytes 983048 | tf_op jit(solution)/shard_map/ppermute | solution.py:351
  8.6 27.8 %collective-permute-start.4 = (bf16[256,640]{1,0:T(8,128)(2,1)S(1)}, bf16[256,640]{1,0:T(8,128)(2,1)S(1)}, u32[]{:S(2)}, u32[]{:S(2)}) collective-permute-start(bf16[256,640]{1,0:T(8,128)(2,1)S(1)} %pad_maximum_fusion.12.refs_0_), channel_id=1, source_target_pairs={{0,4},{4,0},{1,5},{5,1},{2,6},{6,2},{3,7},{7,3},{8,12},{12,8},{9,1... | collective-permute-start | bytes 983048 | tf_op jit(solution)/shard_map/ppermute | solution.py:347
  16.3 21.6 %collective-permute-start.8 = (bf16[256,640]{1,0:T(8,128)(2,1)S(1)}, bf16[256,640]{1,0:T(8,128)(2,1)S(1)}, u32[]{:S(2)}, u32[]{:S(2)}) collective-permute-start(bf16[256,640]{1,0:T(8,128)(2,1)S(1)} %pad_maximum_fusion.12.refs_0_), channel_id=1, source_target_pairs={{0,2},{2,0},{1,3},{3,1},{4,6},{6,4},{5,7},{7,5},{8,10},{10,8},{9,1... | collective-permute-start | bytes 983048 | tf_op jit(solution)/shard_map/ppermute | solution.py:347
  46.5 20.3 %collective-permute-start.16 = (bf16[240,640]{1,0:T(8,128)(2,1)S(1)}, bf16[240,640]{1,0:T(8,128)(2,1)S(1)}, u32[]{:S(2)}, u32[]{:S(2)}) collective-permute-start(bf16[240,640]{1,0:T(8,128)(2,1)S(1)} %pad_maximum_fusion.13.refs_0_), channel_id=1, source_target_pairs={{0,8},{8,16},{16,24},{24,0},{1,9},{9,17},{17,25},{25,1},{2,10},{10... | collective-permute-start | bytes 921608 | tf_op jit(solution)/shard_map/ppermute | solution.py:351
  55.9 21.3 %collective-permute-start.18 = (bf16[240,640]{1,0:T(8,128)(2,1)S(1)}, bf16[240,640]{1,0:T(8,128)(2,1)S(1)}, u32[]{:S(2)}, u32[]{:S(2)}) collective-permute-start(bf16[240,640]{1,0:T(8,128)(2,1)S(1)} %pad_maximum_fusion.13.refs_0_), channel_id=1, source_target_pairs={{0,16},{8,24},{16,0},{24,8},{1,17},{9,25},{17,1},{25,9},{2,18},{10... | collective-permute-start | bytes 921608 | tf_op jit(solution)/shard_map/ppermute | solution.py:351
  161.3 97.5 %collective-permute-start.57 = (bf16[4,2,80,640]{3,2,0,1:T(8,128)(2,1)}, bf16[4,2,80,640]{3,2,0,1:T(8,128)(2,1)}, u32[]{:S(2)}, u32[]{:S(2)}) collective-permute-start(bf16[4,2,80,640]{3,2,0,1:T(8,128)(2,1)} %fusion.84), channel_id=1, source_target_pairs={{0,2},{2,0},{1,3},{3,1},{4,6},{6,4},{5,7},{7,5},{8,10},{10,8},{9,1... | collective-permute-start | bytes 2457608 | tf_op jit(solution)/shard_map/ppermute | solution.py:347
  162.3 140.0 %collective-permute-start.56 = (bf16[4,2,80,640]{3,2,0,1:T(8,128)(2,1)}, bf16[4,2,80,640]{3,2,0,1:T(8,128)(2,1)}, u32[]{:S(2)}, u32[]{:S(2)}) collective-permute-start(bf16[4,2,80,640]{3,2,0,1:T(8,128)(2,1)} %fusion.83), channel_id=1, source_target_pairs={{0,2},{2,0},{1,3},{3,1},{4,6},{6,4},{5,7},{7,5},{8,10},{10,8},{9,1... | collective-permute-start | bytes 2457608 | tf_op jit(solution)/shard_map/ppermute | solution.py:347
  163.8 89.2 %collective-permute-start.60 = (bf16[4,2,80,640]{3,2,0,1:T(8,128)(2,1)}, bf16[4,2,80,640]{3,2,0,1:T(8,128)(2,1)}, u32[]{:S(2)}, u32[]{:S(2)}) collective-permute-start(bf16[4,2,80,640]{3,2,0,1:T(8,128)(2,1)} %fusion.85), channel_id=1, source_target_pairs={{0,2},{2,0},{1,3},{3,1},{4,6},{6,4},{5,7},{7,5},{8,10},{10,8},{9,1... | collective-permute-start | bytes 2457608 | tf_op jit(solution)/shard_map/ppermute | solution.py:347
  164.8 89.9 %collective-permute-start.62 = (bf16[4,2,80,640]{3,2,0,1:T(8,128)(2,1)}, bf16[4,2,80,640]{3,2,0,1:T(8,128)(2,1)}, u32[]{:S(2)}, u32[]{:S(2)}) collective-permute-start(bf16[4,2,80,640]{3,2,0,1:T(8,128)(2,1)} %fusion.86), channel_id=1, source_target_pairs={{0,2},{2,0},{1,3},{3,1},{4,6},{6,4},{5,7},{7,5},{8,10},{10,8},{9,1... | collective-permute-start | bytes 2457608 | tf_op jit(solution)/shard_map/ppermute | solution.py:347
  177.2 83.8 %collective-permute-start.66 = (bf16[4,2,80,640]{3,2,0,1:T(8,128)(2,1)}, bf16[4,2,80,640]{3,2,0,1:T(8,128)(2,1)}, u32[]{:S(2)}, u32[]{:S(2)}) collective-permute-start(bf16[4,2,80,640]{3,2,0,1:T(8,128)(2,1)} %fusion.88), channel_id=1, source_target_pairs={{0,2},{2,0},{1,3},{3,1},{4,6},{6,4},{5,7},{7,5},{8,10},{10,8},{9,1... | collective-permute-start | bytes 2457608 | tf_op jit(solution)/shard_map/ppermute | solution.py:347
  253.0 54.2 %collective-permute-start.65 = (bf16[4,2,80,640]{3,2,0,1:T(8,128)(2,1)S(1)}, bf16[4,2,80,640]{3,2,0,1:T(8,128)(2,1)S(1)}, u32[]{:S(2)}, u32[]{:S(2)}) collective-permute-start(bf16[4,2,80,640]{3,2,0,1:T(8,128)(2,1)S(1)} %copy-done.57), channel_id=1, source_target_pairs={{0,2},{2,0},{1,3},{3,1},{4,6},{6,4},{5,7},{7,5},{8,10},{10,8},{9,1... | collective-permute-start | bytes 2457608 | tf_op jit(solution)/shard_map/ppermute | solution.py:347
  258.8 47.1 %collective-permute-start.51 = (bf16[4,2,80,1920]{3,2,0,1:T(8,128)(2,1)S(1)}, bf16[4,2,80,1920]{3,2,0,1:T(8,128)(2,1)S(1)}, u32[]{:S(2)}, u32[]{:S(2)}) collective-permute-start(bf16[4,2,80,1920]{3,2,0,1:T(8,128)(2,1)S(1)} %fusion.7), channel_id=1, source_target_pairs={{0,2},{2,0},{1,3},{3,1},{4,6},{6,4},{5,7},{7,5},{8,10},{10,8},{9,1... | collective-permute-start | bytes 7372808 | tf_op jit(solution)/shard_map/ppermute | solution.py:347
  260.9 43.0 %collective-permute-start.58 = (bf16[4,2,80,640]{3,2,0,1:T(8,128)(2,1)S(1)}, bf16[4,2,80,640]{3,2,0,1:T(8,128)(2,1)S(1)}, u32[]{:S(2)}, u32[]{:S(2)}) collective-permute-start(bf16[4,2,80,640]{3,2,0,1:T(8,128)(2,1)S(1)} %fusion.10), channel_id=1, source_target_pairs={{0,1},{1,0},{2,3},{3,2},{4,5},{5,4},{6,7},{7,6},{8,9},{9,8},{10,11... | collective-permute-start | bytes 2457608 | tf_op jit(solution)/shard_map/ppermute | solution.py:347
  300.8 23.7 %collective-permute-start.61 = (bf16[4,80,640]{2,1,0:T(8,128)(2,1)S(1)}, bf16[4,80,640]{2,1,0:T(8,128)(2,1)S(1)}, u32[]{:S(2)}, u32[]{:S(2)}) collective-permute-start(bf16[4,80,640]{2,1,0:T(8,128)(2,1)S(1)} %fusion.99), channel_id=1, source_target_pairs={{0,4},{4,0},{1,5},{5,1},{2,6},{6,2},{3,7},{7,3},{8,12},{12,8},{9,1... | collective-permute-start | bytes 1228808 | tf_op jit(solution)/shard_map/ppermute | solution.py:347
  302.3 21.2 %collective-permute-start.67 = (bf16[4,2,80,640]{3,2,0,1:T(8,128)(2,1)S(1)}, bf16[4,2,80,640]{3,2,0,1:T(8,128)(2,1)S(1)}, u32[]{:S(2)}, u32[]{:S(2)}) collective-permute-start(bf16[4,2,80,640]{3,2,0,1:T(8,128)(2,1)S(1)} %fusion.8), channel_id=1, source_target_pairs={{0,1},{1,0},{2,3},{3,2},{4,5},{5,4},{6,7},{7,6},{8,9},{9,8},{10,11... | collective-permute-start | bytes 2457608 | tf_op jit(solution)/shard_map/ppermute | solution.py:347
  303.9 25.5 %collective-permute-start.64 = (bf16[4,80,640]{2,1,0:T(8,128)(2,1)S(1)}, bf16[4,80,640]{2,1,0:T(8,128)(2,1)S(1)}, u32[]{:S(2)}, u32[]{:S(2)}) collective-permute-start(bf16[4,80,640]{2,1,0:T(8,128)(2,1)S(1)} %fusion.89), channel_id=1, source_target_pairs={{0,1},{1,0},{2,3},{3,2},{4,5},{5,4},{6,7},{7,6},{8,9},{9,8},{10,11... | collective-permute-start | bytes 1228808 | tf_op jit(solution)/shard_map/ppermute | solution.py:347
  305.9 23.6 %collective-permute-start.59 = (bf16[4,80,640]{2,1,0:T(8,128)(2,1)S(1)}, bf16[4,80,640]{2,1,0:T(8,128)(2,1)S(1)}, u32[]{:S(2)}, u32[]{:S(2)}) collective-permute-start(bf16[4,80,640]{2,1,0:T(8,128)(2,1)S(1)} %fusion.98), channel_id=1, source_target_pairs={{0,4},{4,0},{1,5},{5,1},{2,6},{6,2},{3,7},{7,3},{8,12},{12,8},{9,1... | collective-permute-start | bytes 1228808 | tf_op jit(solution)/shard_map/ppermute | solution.py:347
  307.2 51.9 %collective-permute-start.52 = (bf16[4,80,1920]{2,1,0:T(8,128)(2,1)S(1)}, bf16[4,80,1920]{2,1,0:T(8,128)(2,1)S(1)}, u32[]{:S(2)}, u32[]{:S(2)}) collective-permute-start(bf16[4,80,1920]{2,1,0:T(8,128)(2,1)S(1)} %fusion.67), channel_id=1, source_target_pairs={{0,4},{4,0},{1,5},{5,1},{2,6},{6,2},{3,7},{7,3},{8,12},{12,8},{9,1... | collective-permute-start | bytes 3686408 | tf_op jit(solution)/shard_map/ppermute | solution.py:347
  323.8 30.9 %collective-permute-start.68 = (bf16[4,80,640]{2,1,0:T(8,128)(2,1)S(1)}, bf16[4,80,640]{2,1,0:T(8,128)(2,1)S(1)}, u32[]{:S(2)}, u32[]{:S(2)}) collective-permute-start(bf16[4,80,640]{2,1,0:T(8,128)(2,1)S(1)} %fusion.101), channel_id=1, source_target_pairs={{0,4},{4,0},{1,5},{5,1},{2,6},{6,2},{3,7},{7,3},{8,12},{12,8},{9,1... | collective-permute-start | bytes 1228808 | tf_op jit(solution)/shard_map/ppermute | solution.py:347
  355.4 24.1 %collective-permute-start.70 = (bf16[240,640]{1,0:T(8,128)(2,1)S(1)}, bf16[240,640]{1,0:T(8,128)(2,1)S(1)}, u32[]{:S(2)}, u32[]{:S(2)}) collective-permute-start(bf16[240,640]{1,0:T(8,128)(2,1)S(1)} %get-tuple-element.90), channel_id=1, source_target_pairs={{0,24},{8,0},{16,8},{24,16},{1,25},{9,1},{17,9},{25,17},{2,26},{10... | collective-permute-start | bytes 921608 | tf_op jit(solution)/shard_map/ppermute | solution.py:351
  359.0 38.0 %collective-permute-start.71 = (bf16[240,640]{1,0:T(8,128)(2,1)S(1)}, bf16[240,640]{1,0:T(8,128)(2,1)S(1)}, u32[]{:S(2)}, u32[]{:S(2)}) collective-permute-start(bf16[240,640]{1,0:T(8,128)(2,1)S(1)} %get-tuple-element.89), channel_id=1, source_target_pairs={{0,16},{8,24},{16,0},{24,8},{1,17},{9,25},{17,1},{25,9},{2,18},{10... | collective-permute-start | bytes 921608 | tf_op jit(solution)/shard_map/ppermute | solution.py:351
  359.4 38.6 %collective-permute-start.53 = (bf16[80,1920]{1,0:T(8,128)(2,1)S(1)}, bf16[80,1920]{1,0:T(8,128)(2,1)S(1)}, u32[]{:S(2)}, u32[]{:S(2)}) collective-permute-start(bf16[80,1920]{1,0:T(8,128)(2,1)S(1)} %get-tuple-element.91), channel_id=1, source_target_pairs={{0,8},{8,16},{16,24},{24,0},{1,9},{9,17},{17,25},{25,1},{2,10},{10... | collective-permute-start | bytes 921608 | tf_op jit(solution)/shard_map/ppermute | solution.py:351
  360.5 37.5 %collective-permute-start.54 = (bf16[80,1920]{1,0:T(8,128)(2,1)S(1)}, bf16[80,1920]{1,0:T(8,128)(2,1)S(1)}, u32[]{:S(2)}, u32[]{:S(2)}) collective-permute-start(bf16[80,1920]{1,0:T(8,128)(2,1)S(1)} %get-tuple-element.93), channel_id=1, source_target_pairs={{0,24},{8,0},{16,8},{24,16},{1,25},{9,1},{17,9},{25,17},{2,26},{10... | collective-permute-start | bytes 921608 | tf_op jit(solution)/shard_map/ppermute | solution.py:351
  367.2 41.8 %collective-permute-start.55 = (bf16[80,1920]{1,0:T(8,128)(2,1)S(1)}, bf16[80,1920]{1,0:T(8,128)(2,1)S(1)}, u32[]{:S(2)}, u32[]{:S(2)}) collective-permute-start(bf16[80,1920]{1,0:T(8,128)(2,1)S(1)} %get-tuple-element.92), channel_id=1, source_target_pairs={{0,16},{8,24},{16,0},{24,8},{1,17},{9,25},{17,1},{25,9},{2,18},{10... | collective-permute-start | bytes 921608 | tf_op jit(solution)/shard_map/ppermute | solution.py:351
  (137 other events, 1168.6 us)
